TPU v7x, 256 devices: a whole 4x4x8 slice. The times are simulated.
256 devices in a mesh: tensor: 2 (over x_lo), node: 16 (over x_hi, z), local: 8 (over y, core).
Axes of the slice: x: 4 (x_hi: 2, x_lo: 2; x = x_hi * 2 + x_lo), y: 4, z: 8, core: 2. Of those that a mesh axis runs over, the one named last changes fastest.
Arguments:
- acts: bfloat16 [16384, 6144], P(('node', 'local')), may hold values from -0.1875 to 0.1875
- grad_q: bfloat16 [16384, 6144], P(('node', 'local'), 'tensor'), may hold values from -6 to 6
- weight_q: bfloat16 [6144, 6144], P('local', 'tensor'), may hold values from -0.078125 to 0.078125
Outputs:
- weight_grad: float32 [8, 768, 6144], P('local', 'node', 'tensor')
- act_grad: bfloat16 [16384, 6144], P(('node', 'local'))
All inputs are finite; a program needn't handle non-finite values.
Results may differ from a plain program's by a relative error of at most 0.001.
Values may be sent and summed in bfloat16 or wider, within the bound.
A program may use at most 128 MiB of HBM per device.

v0:
```python
import jax
import jax.numpy as jnp
from jax import lax
from jax.sharding import PartitionSpec as P


def on_device(acts, grad_q, weight_q):
    pieces = lax.all_to_all(acts, "local", split_axis=1, concat_axis=0, tiled=True)
    group_grads = lax.all_gather(grad_q, "local", axis=0, tiled=True)
    partial_value = lax.dot_general(
        pieces, group_grads, (((0,), (0,)), ((), ())), preferred_element_type=jnp.float32
    )
    summed_rows = lax.psum_scatter(partial_value, "node", scatter_dimension=0, tiled=True)
    weight_grad = summed_rows[None]
    projected = lax.dot_general(
        group_grads, weight_q, (((1,), (1,)), ((), ())), preferred_element_type=jnp.float32
    )
    returned = lax.all_to_all(projected, "local", split_axis=0, concat_axis=1, tiled=True)
    act_grad = lax.psum(returned, "tensor").astype(jnp.bfloat16)
    return (weight_grad, act_grad)


def solution(mesh):
    placed = (P(("node", "local"), None), P(("node", "local"), "tensor"), P("local", "tensor"))
    return jax.shard_map(
        on_device,
        mesh=mesh,
        in_specs=placed,
        out_specs=(P("local", "node", "tensor"), P(("node", "local"), None)),
        check_vma=False,
    )
```

profile of v0, /device:TPU:1, one launch (start us, length us, event | category | flops | bytes accessed | tf_op | source)
XLA Modules:
  0.0 329.5 jit_solution(16316121900015981170)
XLA Ops:
  7.2 0.0 all-gather.2.cloned.1.call-start
  7.2 0.7 all-gather.2.cloned.1.call-update
  7.9 0.0 reduce-scatter.2.cloned.1.call-start
  7.9 1.9 copy.7
  9.9 32.4 %all_to_all.38 = bf16[128,8,768]{0,2,1:T(8,128)(2,1)S(1)} all-to-all(bf16[128,8,768]{0,2,1:T(8,128)(2,1)S(1)} %bitcast.15), channel_id=1, replica_groups=mesh['tensor'=2,'node'=16,'local'=8] {'local'}, dimensions={1} | all-to-all | bytes 3145728 | tf_op jit(solution)/shard_map/all_to_all | solution.py:8
  42.3 0.7 copy.8
  43.0 20.7 %all-gather.2.cloned.1.call-done = bf16[1024,3072]{1,0:T(8,128)(2,1)} async-done(((bf16[128,3072]{1,0:T(8,128)(2,1)}), bf16[1024,3072]{1,0:T(8,128)(2,1)}) %all-gather.2.cloned.1.call-update) | async-done | bytes 6291472 | tf_op jit(solution)/shard_map/all_gather | solution.py:9
  63.7 10.3 %fusion = f32[768,3072]{1,0:T(8,128)} fusion(bf16[1024,768]{1,0:T(8,128)(2,1)S(1)} %bitcast.17, bf16[1024,3072]{1,0:T(8,128)(2,1)} %all-gather.2.cloned.1.call-done), kind=kOutput, calls=%fused_computation | convolution fusion | flops 4831838208 | bytes 17301504 | tf_op jit(solution)/shard_map/dot_general | solution.py:10
  74.0 0.0 reduce-scatter.2.cloned.1.call-update
  74.0 8.6 %fusion.1 = f32[1024,768]{1,0:T(8,128)S(1)} fusion(bf16[1024,3072]{1,0:T(8,128)(2,1)} %all-gather.2.cloned.1.call-done, bf16[768,3072]{1,0:T(8,128)(2,1)} %param.5), kind=kOutput, calls=%fused_computation.1 | convolution fusion | flops 4831838208 | bytes 14155776 | tf_op jit(solution)/shard_map/dot_general | solution.py:15
  82.6 40.7 %all_to_all.39 = f32[8,128,768]{2,1,0:T(8,128)S(1)} all-to-all(f32[8,128,768]{2,1,0:T(8,128)S(1)} %bitcast.16), channel_id=1, replica_groups=mesh['tensor'=2,'node'=16,'local'=8] {'local'}, dimensions={0} | all-to-all | bytes 6291456 | tf_op jit(solution)/shard_map/all_to_all | solution.py:18
  123.3 0.3 copy.10
  123.7 93.3 %all-reduce.1 = bf16[128,6144]{1,0:T(8,128)(2,1)} all-reduce(f32[128,6144]{1,0:T(8,128)S(1)} %bitcast.13), channel_id=1, replica_groups=mesh['tensor'=2,'node'=16,'local'=8] {'tensor'}, use_global_device_ids=true, to_apply=%region_1.0 | all-reduce | flops 786432 | bytes 4718592 | tf_op jit(solution)/shard_map/psum | solution.py:19
  216.9 105.8 %reduce-scatter.2.cloned.1.call-done = f32[48,3072]{1,0:T(8,128)} async-done(((f32[768,3072]{1,0:T(8,128)}), f32[48,3072]{1,0:T(8,128)}) %reduce-scatter.2.cloned.1.call-update) | async-done | bytes 589840 | tf_op jit(solution)/shard_map/reduce_scatter | solution.py:13
Async XLA Ops:
  7.2 56.5 %all-gather.2.cloned.1.call-start = ((), (), s32[]{:S(2)}) async-start(), calls=%async_computation.3 | async-start | bytes 7077888 | tf_op jit(solution)/shard_map/all_gather | solution.py:9
  7.9 314.8 %reduce-scatter.2.cloned.1.call-start = ((), (), s32[]{:S(2)}) async-start(), calls=%async_computation.4 | async-start | bytes 10027008 | tf_op jit(solution)/shard_map/reduce_scatter | solution.py:13
Sparse Core Ops, SparseCore 0:
  9.8 53.8 all-gather.1
  74.1 248.4 reduce-scatter.1
where the time goes:
time: 333 us; the launch traced here: 330 us
  blocking collectives  166 us (50%)
  waiting for transfers between devices  127 us (38%)
  matrix products  18.9 us (6%)
  between operations  14.1 us (4%)
    reduce_scatter x1, waiting for transfers between devices, on_device(): lax.psum_scatter(partial_value, 'node', scatter_dimension=0, tiled=True)  106 us
    psum x1, blocking collectives, on_device(): act_grad = lax.psum(returned, 'tensor').astype(jnp.bfloat16)  93.3 us
    all_to_all x1, blocking collectives, on_device(): lax.all_to_all(projected, 'local', split_axis=0, concat_axis=1, tiled=True)  40.7 us
    all_to_all x1, blocking collectives, on_device(): lax.all_to_all(acts, 'local', split_axis=1, concat_axis=0, tiled=True)  32.4 us
    all_gather x1, waiting for transfers between devices, on_device(): group_grads = lax.all_gather(grad_q, 'local', axis=0, tiled=True)  20.7 us
    dot_general x1, matrix products, on_device(): lax.dot_general(pieces, group_grads, (((0,), (0,)), ((), ())), preferred_...  10.3 us
    dot_general x1, matrix products, on_device(): lax.dot_general(group_grads, weight_q, (((1,), (1,)), ((), ())), preferre...  8.61 us
  transfers between devices with their start and end apart: 2, of which 2 were waited for; matrix products, arithmetic and copies ran while one was open for 4% of the time, Pallas kernels for 0%

commit v1 on v0

v1 whole, which is shorter than its diff:
```python
import functools

import jax
import jax.numpy as jnp
from jax import lax
from jax.experimental import pallas as pl
from jax.experimental.pallas import tpu as pltpu
from jax.sharding import PartitionSpec as P

MESH = pl.DeviceIdType.MESH
F32, BF16 = jnp.float32, jnp.bfloat16

TOK = 128
D_BLK = 768
HALF = 384
QL = 3072
CW = 768
NK = QL // CW
ROWS = 48
NU = 2 * NK

Z_SCALE = 128.0
X_SCALE = 64.0


def power_code(v, scale):
    v = v * scale
    v2 = v * v
    v4 = v2 * v2
    return (v4 * v2 * v).astype(BF16)


def power_value(code, scale):
    c = code.astype(F32)
    root = jnp.exp(jnp.log(jnp.maximum(jnp.abs(c), 1e-38)) * (1.0 / 7.0)) * (1.0 / scale)
    root = jnp.where(jnp.abs(c) < 1e-37, 0.0, root)
    return jnp.where(c < 0, -root, root)


def kernel(
    acts, grads, wq, wg_out, ag_out,
    W, G, A, AT, PZ, PX, zs, zr, xs, xr, hs, hr, fin,
    loc_sem, sib_sem, a_ss, a_rs, g_ss, g_rs, z_ss, z_rs, x_ss, x_rs, h_ss, h_rs,
    o_ss, o_rs, ag_ss, ag_rs,
):
    t = lax.axis_index("tensor")
    n = lax.axis_index("node")
    l = lax.axis_index("local")
    xh, z = n // 8, n % 8
    y, c = l // 2, l % 2
    yp, ym, y2 = (y + 1) % 4, (y + 3) % 4, (y + 2) % 4

    def at_local(l_):
        return (t, n, l_)

    sib = at_local(y * 2 + 1 - c)
    dev_yp, dev_ym = at_local(yp * 2 + c), at_local(ym * 2 + c)
    dev_z = (
        (t, xh * 8 + (z + 1) % 8, l),
        (t, xh * 8 + (z + 7) % 8, l),
    )
    dev_h = (t, (1 - xh) * 8 + z, l)
    dev_x = (1 - t, n, l)

    started = []

    def send(src, dst, ss, rs, dev):
        cp = pltpu.make_async_remote_copy(
            src_ref=src, dst_ref=dst, send_sem=ss, recv_sem=rs, device_id=dev, device_id_type=MESH
        )
        cp.start()
        started.append(cp)

    def arrived(dst, rs):
        pltpu.make_async_remote_copy(
            src_ref=dst, dst_ref=dst, send_sem=rs, recv_sem=rs, device_id=sib, device_id_type=MESH
        ).wait_recv()

    barrier = pltpu.get_barrier_semaphore()
    partners = [at_local((l + o) % 8) for o in range(1, 8)] + [dev_z[0], dev_z[1], dev_h, dev_x]
    for dev in partners:
        pl.semaphore_signal(barrier, inc=1, device_id=dev, device_id_type=MESH)
    pl.semaphore_wait(barrier, len(partners))

    def cols(k):
        return pl.ds(k * CW, CW)

    def acts_cols(l_, hf):
        h = (1 - xh) if hf == 0 else xh
        return pl.ds(pl.multiple_of(l_ * D_BLK + h * HALF, 128), HALF)

    def out_cols(l_, t_):
        return pl.ds(pl.multiple_of(l_ * D_BLK + t_ * HALF, 128), HALF)

    local = [
        pltpu.make_async_copy(grads, G.at[l], loc_sem.at[0]),
        pltpu.make_async_copy(wq, W, loc_sem.at[1]),
        pltpu.make_async_copy(acts.at[:, acts_cols(l, 0)], A.at[0, l], loc_sem.at[2]),
        pltpu.make_async_copy(acts.at[:, acts_cols(l, 1)], A.at[1, l], loc_sem.at[3]),
    ]

    def send_acts(hf):
        for o in (4, 5, 3, 2, 6, 7, 1):
            l_ = (l + o) % 8
            send(acts.at[:, acts_cols(l_, hf)], A.at[hf, l], a_ss.at[hf, o], a_rs.at[hf, o], at_local(l_))

    def take_acts(hf):
        for o in range(1, 8):
            arrived(A.at[hf, (l + 8 - o) % 8], a_rs.at[hf, o])
        for i in range(8):
            AT[hf, :, i * TOK : (i + 1) * TOK] = A[hf, i].T

    def send_own(k):
        src = grads.at[:, cols(k)]
        send(src, G.at[l, :, cols(k)], g_ss.at[k, 0], g_rs.at[k, 0], dev_yp)
        send(src, G.at[l, :, cols(k)], g_ss.at[k, 1], g_rs.at[k, 1], dev_ym)

    def relay(k):
        lm, lp = ym * 2 + c, yp * 2 + c
        below, above = G.at[lm, :, cols(k)], G.at[lp, :, cols(k)]
        arrived(below, g_rs.at[k, 0])
        low = G.at[lm, pl.ds(0, TOK // 2), cols(k)]
        send(low, low, g_ss.at[k, 2], g_rs.at[k, 2], dev_yp)
        arrived(above, g_rs.at[k, 1])
        high = G.at[lp, pl.ds(TOK // 2, TOK // 2), cols(k)]
        send(high, high, g_ss.at[k, 3], g_rs.at[k, 3], dev_ym)
        send(below, below, g_ss.at[k, 4], g_rs.at[k, 4], sib)
        send(above, above, g_ss.at[k, 5], g_rs.at[k, 5], sib)

    def complete(k):
        lf = y2 * 2 + c
        arrived(G.at[lf, pl.ds(0, TOK // 2), cols(k)], g_rs.at[k, 2])
        arrived(G.at[lf, pl.ds(TOK // 2, TOK // 2), cols(k)], g_rs.at[k, 3])
        far = G.at[lf, :, cols(k)]
        send(far, far, g_ss.at[k, 6], g_rs.at[k, 6], sib)
        arrived(G.at[ym * 2 + 1 - c, :, cols(k)], g_rs.at[k, 4])
        arrived(G.at[yp * 2 + 1 - c, :, cols(k)], g_rs.at[k, 5])
        arrived(G.at[y2 * 2 + 1 - c, :, cols(k)], g_rs.at[k, 6])

    def unit_block(u):
        hf, k = divmod(u, NK)

        @pl.loop(0, CW // 256)
        def _(i):
            at = pl.multiple_of(k * CW + i * 256, 128)
            g = G[:, :, pl.ds(at, 256)].reshape(8 * TOK, 256)
            PZ[u, :, pl.ds(pl.multiple_of(i * 256, 128), 256)] = jnp.dot(
                AT[hf], g, preferred_element_type=F32
            )

    def steps_of(u, d):
        return (1, 2, 3, 4) if u % 2 == d else (2, 3, 4)

    def z_step(u, s):
        for d in range(2):
            if s not in steps_of(u, d):
                continue
            first = s == steps_of(u, d)[0]
            to = (z + 5 - s) % 8 if d == 0 else (z + 3 + s) % 8
            if not first:
                arrived(zr.at[u, d, s - 2], z_rs.at[u, d, s - 2])

            @pl.loop(0, ROWS // 16)
            def _(i):
                r = pl.ds(pl.multiple_of(i * 16, 16), 16)
                v = PZ[u, pl.ds(pl.multiple_of(to * ROWS + i * 16, 16), 16), :]
                if not first:
                    v = v + power_value(zr[u, d, s - 2, r, :], Z_SCALE)
                zs[u, d, s - 1, r, :] = power_code(v, Z_SCALE)

            send(zs.at[u, d, s - 1], zr.at[u, d, s - 1], z_ss.at[u, d, s - 1], z_rs.at[u, d, s - 1], dev_z[d])

    def z_final(u):
        hf, k = divmod(u, NK)
        for d in range(2):
            arrived(zr.at[u, d, 3], z_rs.at[u, d, 3])
        if hf == 1:
            arrived(hr.at[k], h_rs.at[k])

        @pl.loop(0, ROWS // 16)
        def _(i):
            r = pl.ds(pl.multiple_of(i * 16, 16), 16)
            v = PZ[u, pl.ds(pl.multiple_of(z * ROWS + i * 16, 16), 16), :]
            v = v + power_value(zr[u, 0, 3, r, :], Z_SCALE) + power_value(zr[u, 1, 3, r, :], Z_SCALE)
            if hf == 0:
                hs[k, r, :] = power_code(v, Z_SCALE)
            else:
                wg_out[0, r, cols(k)] = v + power_value(hr[k, r, :], Z_SCALE)

        if hf == 0:
            send(hs.at[k], hr.at[k], h_ss.at[k], h_rs.at[k], dev_h)

    chip = (y, yp, ym, y2)

    def x_add(b, k, first):
        yb = chip[b]

        @pl.loop(0, 2)
        def _(i):
            g = G[yb * 2 + i, :, cols(k)]
            p = lax.dot_general(g, W[:, cols(k)], (((1,), (1,)), ((), ())), preferred_element_type=F32)
            r = pl.ds(pl.multiple_of(i * TOK, TOK), TOK)
            PX[b, r, :] = p if first else PX[b, r, :] + p

    def x_send(b):
        theirs = pl.ds(pl.multiple_of((1 - t) * HALF, 128), HALF)

        @pl.loop(0, 2 * TOK // 32)
        def _(i):
            r = pl.ds(pl.multiple_of(i * 32, 32), 32)
            xs[b, r, :] = power_code(PX[b, r, theirs], X_SCALE)

        send(xs.at[b], xr.at[b], x_ss.at[b], x_rs.at[b], dev_x)

    def x_final(b):
        arrived(xr.at[b], x_rs.at[b])
        mine = pl.ds(pl.multiple_of(t * HALF, 128), HALF)

        @pl.loop(0, 2 * TOK // 32)
        def _(i):
            r = pl.ds(pl.multiple_of(i * 32, 32), 32)
            fin[b, r, :] = (PX[b, r, mine] + power_value(xr[b, r, :], X_SCALE)).astype(BF16)

        if b == 0:
            own = pl.ds(pl.multiple_of(c * TOK, TOK), TOK)
            other = pl.ds(pl.multiple_of((1 - c) * TOK, TOK), TOK)
            cp = pltpu.make_async_copy(fin.at[0, own], ag_out.at[:, out_cols(l, t)], loc_sem.at[4])
            cp.start()
            local.append(cp)
            send(fin.at[0, own], ag_out.at[:, out_cols(l, t)], ag_ss.at[0], ag_rs.at[0], dev_x)
            send(fin.at[0, other], ag_out.at[:, out_cols(l, t)], o_ss.at[0], o_rs.at[1], sib)
        else:
            for i in range(2):
                there = {1: 2, 2: 1, 3: 3}[b]
                send(
                    fin.at[b, pl.ds(i * TOK, TOK)], ag_out.at[:, out_cols(l, t)],
                    o_ss.at[2 * b + i], o_rs.at[2 * there + c], at_local(chip[b] * 2 + i),
                )

    def x_share(b):
        for i in range(2):
            if b == 0 and i == 0:
                continue
            l_ = (y * 2 + 1 - c) if b == 0 else chip[b] * 2 + i
            piece = ag_out.at[:, out_cols(l_, t)]
            arrived(piece, o_rs.at[2 * b + i])
            send(piece, piece, ag_ss.at[2 * b + i], ag_rs.at[2 * b + i], dev_x)

    local[0].start()
    local[1].start()
    send(grads, G.at[l], sib_sem.at[0], sib_sem.at[1], sib)
    send_own(0)
    local[2].start()
    send_acts(0)
    local[3].start()
    local[0].wait()
    local[1].wait()
    arrived(G.at[y * 2 + 1 - c], sib_sem.at[1])
    for k in range(NK):
        x_add(0, k, k == 0)
    x_send(0)
    relay(0)
    send_own(1)
    x_final(0)
    local[2].wait()
    take_acts(0)
    complete(0)
    for slot in range(NU + 5):
        u = slot
        if u < NK:
            if u + 2 < NK:
                send_own(u + 2)
            if u == 2:
                send_acts(1)
        if u == NK:
            local[3].wait()
            take_acts(1)
        if u < NU:
            unit_block(u)
            z_step(u, 1)
        if u < NK:
            if u + 1 < NK:
                relay(u + 1)
            for b in (1, 2, 3):
                x_add(b, u, u == 0)
                if u == NK - 1:
                    x_send(b)
        for s in (2, 3, 4):
            if 0 <= u - (s - 1) < NU:
                z_step(u - (s - 1), s)
        if 0 <= u - 4 < NU:
            z_final(u - 4)
        if u == 0:
            x_share(0)
        if u + 1 < NK:
            complete(u + 1)
        if u == NK:
            for b in (1, 2, 3):
                x_final(b)
        if u == NK + 1:
            for b in (1, 2, 3):
                x_share(b)
    for b in range(4):
        for i in range(2):
            l_ = (l if i == 0 else y * 2 + 1 - c) if b == 0 else chip[b] * 2 + i
            arrived(ag_out.at[:, out_cols(l_, 1 - t)], ag_rs.at[2 * b + i])
    local[4].wait()
    for cp in started:
        cp.wait_send()


def on_device(acts, grad_q, weight_q):
    dma = pltpu.SemaphoreType.DMA
    return pl.pallas_call(
        kernel,
        out_shape=(
            jax.ShapeDtypeStruct((1, ROWS, QL), F32),
            jax.ShapeDtypeStruct((TOK, 8 * D_BLK), BF16),
        ),
        in_specs=[pl.BlockSpec(memory_space=pl.ANY)] * 3,
        out_specs=(pl.BlockSpec(memory_space=pltpu.VMEM), pl.BlockSpec(memory_space=pl.ANY)),
        scratch_shapes=[
            pltpu.VMEM((D_BLK, QL), BF16),
            pltpu.VMEM((8, TOK, QL), BF16),
            pltpu.VMEM((2, 8, TOK, HALF), BF16),
            pltpu.VMEM((2, HALF, 8 * TOK), BF16),
            pltpu.VMEM((NU, HALF, CW), F32),
            pltpu.VMEM((4, 2 * TOK, D_BLK), F32),
            pltpu.VMEM((NU, 2, 4, ROWS, CW), BF16),
            pltpu.VMEM((NU, 2, 4, ROWS, CW), BF16),
            pltpu.VMEM((4, 2 * TOK, HALF), BF16),
            pltpu.VMEM((4, 2 * TOK, HALF), BF16),
            pltpu.VMEM((NK, ROWS, CW), BF16),
            pltpu.VMEM((NK, ROWS, CW), BF16),
            pltpu.VMEM((4, 2 * TOK, HALF), BF16),
            dma((5,)),
            dma((2,)),
            dma((2, 8)),
            dma((2, 8)),
            dma((NK, 7)),
            dma((NK, 7)),
            dma((NU, 2, 4)),
            dma((NU, 2, 4)),
            dma((4,)),
            dma((4,)),
            dma((NK,)),
            dma((NK,)),
            dma((8,)),
            dma((8,)),
            dma((8,)),
            dma((8,)),
        ],
        compiler_params=pltpu.CompilerParams(
            collective_id=0, has_side_effects=True, vmem_limit_bytes=56 * 2**20
        ),
        name="projection_backward",
    )(acts, grad_q, weight_q)


def solution(mesh):
    placed = (P(("node", "local"), None), P(("node", "local"), "tensor"), P("local", "tensor"))
    return jax.shard_map(
        on_device,
        mesh=mesh,
        in_specs=placed,
        out_specs=(P("local", "node", "tensor"), P(("node", "local"), None)),
        check_vma=False,
    )
```

time: 333 us -> 120 us (0.36)
  blocking collectives: 166 us -> 0 us
  waiting for transfers between devices: 127 us -> 0 us
  Pallas kernels: 0 us -> 114 us
  matrix products: 18.9 us -> 0 us
  between operations: 14.1 us -> 0.64 us
    pallas_call x0 -> x1, Pallas kernels: none -> 114 us  [on_device(): pl.pallas_call(kernel, out_shape=(jax.ShapeDtypeStruct((1, ROWS, QL), F32...]
    reduce_scatter x1 -> x0, waiting for transfers between devices: 106 us -> none  [on_device(): lax.psum_scatter(partial_value, 'node', scatter_dimension=0, tiled=True)]
    psum x1 -> x0, blocking collectives: 93.3 us -> none  [on_device(): act_grad = lax.psum(returned, 'tensor').astype(jnp.bfloat16)]
    all_to_all x2 -> x0, blocking collectives: 73.1 us -> none  [the longest x1 40.7 us: on_device(): lax.all_to_all(projected, 'local', split_axis=0, concat_axis=1, tiled=True)]
    all_gather x1 -> x0, waiting for transfers between devices: 20.7 us -> none  [on_device(): group_grads = lax.all_gather(grad_q, 'local', axis=0, tiled=True)]
    dot_general x2 -> x0, matrix products: 18.9 us -> none  [the longest x1 10.3 us: on_device(): lax.dot_general(pieces, group_grads, (((0,), (0,)), ((), ())), preferred_...]
  transfers between devices with their start and end apart: 2 -> 0, of which waited for: 2 -> 0; matrix products, arithmetic and copies ran while one was open for 4% -> 0% of each run, Pallas kernels for 0% -> 0%
where the time goes in v1:
time: 120 us; the launch traced here: 119 us
  Pallas kernels  114 us (95%)
  local copies, waits for them, and re-layouts  4.61 us (4%)
    pallas_call x1, Pallas kernels, on_device(): pl.pallas_call(kernel, out_shape=(jax.ShapeDtypeStruct((1, ROWS, QL), F32...  114 us
    unnamed x2, local copies, waits for them, and re-layouts  4.61 us

profile of v1, /device:TPU:1, one launch (start us, length us, event | category | flops | bytes accessed | tf_op | source)
XLA Modules:
  0.0 119.2 jit_solution(4074205828976066778)
XLA Ops:
  0.6 114.0 %projection_backward.1 = (f32[1,48,3072]{2,1,0:T(8,128)}, bf16[128,6144]{1,0:T(8,128)(2,1)}) custom-call(bf16[128,6144]{1,0:T(8,128)(2,1)} %acts.1, bf16[128,3072]{1,0:T(8,128)(2,1)} %grads.1, bf16[768,3072]{1,0:T(8,128)(2,1)} %wq.1), custom_call_target="tpu_custom_call" | custom-call | tf_op jit(solution)/shard_map/projection_backward/pallas_call | solution.py:314
  114.6 1.9 %copy.7 = f32[1,48,3072]{2,1,0:T(8,128)} copy(f32[1,48,3072]{2,1,0:T(8,128)} %get-tuple-element.4) | data formatting | bytes 1179648
  116.6 2.7 %copy.8 = bf16[128,6144]{1,0:T(8,128)(2,1)} copy(bf16[128,6144]{1,0:T(8,128)(2,1)} %get-tuple-element.5) | data formatting | bytes 3145728

commit v2 on v1

v2 whole, which is shorter than its diff:
```python
import jax
import jax.numpy as jnp
from jax import lax
from jax.experimental import pallas as pl
from jax.experimental.pallas import tpu as pltpu
from jax.sharding import PartitionSpec as P

MESH = pl.DeviceIdType.MESH
F32, BF16 = jnp.float32, jnp.bfloat16

TOK = 128
D_BLK = 768
HALF = 384
QL = 3072
CW = 768
NK = QL // CW
ROWS = 48
NU = 2 * NK

A_NEAR = 80
A_FAR = TOK - A_NEAR

Z_POWER, Z_SCALE = 5, 1024.0
X_POWER, X_TOP = 15, 300.0


def power(v, p):
    out, square = None, v
    while p:
        if p & 1:
            out = square if out is None else out * square
        p >>= 1
        if p:
            square = square * square
    return out


def root(code, p):
    a = jnp.abs(code)
    r = jnp.exp(jnp.log(jnp.maximum(a, 1e-38)) * (1.0 / p))
    r = jnp.where(a < 1e-37, 0.0, r)
    return jnp.where(code < 0, -r, r)


def z_code(v):
    return power(v * Z_SCALE, Z_POWER).astype(BF16)


def z_value(code):
    return root(code.astype(F32), Z_POWER) * (1.0 / Z_SCALE)


def kernel(
    acts, grads, wq, wg_out, ag_out,
    W, G, AS, A, AT, PZ, PX, zs, zr, xs, xr, hs, hr, wo, fin, AO,
    lg_sem, lw_sem, la_sem, lo_sem, lz_sem, sib_sem, a_ss, a_rs, ax_ss, ax_rs, g_ss, g_rs,
    z_ss, z_rs, x_ss, x_rs, h_ss, h_rs, o_ss, o_rs, ag_ss, ag_rs,
):
    t = lax.axis_index("tensor")
    n = lax.axis_index("node")
    l = lax.axis_index("local")
    xh, z = n // 8, n % 8
    y, c = l // 2, l % 2
    yp, ym, y2 = (y + 1) % 4, (y + 3) % 4, (y + 2) % 4
    chip = (y, yp, ym, y2)

    def at_local(l_):
        return (t, n, l_)

    l_sib = y * 2 + 1 - c
    sib = at_local(l_sib)
    dev_yp, dev_ym = at_local(yp * 2 + c), at_local(ym * 2 + c)
    dev_z = (
        (t, xh * 8 + (z + 1) % 8, l),
        (t, xh * 8 + (z + 7) % 8, l),
    )
    dev_h = (t, (1 - xh) * 8 + z, l)
    dev_x = (1 - t, n, l)

    started, stores = [], []

    def send(src, dst, ss, rs, dev):
        cp = pltpu.make_async_remote_copy(
            src_ref=src, dst_ref=dst, send_sem=ss, recv_sem=rs, device_id=dev, device_id_type=MESH
        )
        cp.start()
        started.append(cp)

    def arrived(dst, rs):
        pltpu.make_async_remote_copy(
            src_ref=dst, dst_ref=dst, send_sem=rs, recv_sem=rs, device_id=sib, device_id_type=MESH
        ).wait_recv()

    def store(src, dst, sem):
        cp = pltpu.make_async_copy(src, dst, sem)
        cp.start()
        stores.append(cp)

    def cols(k):
        return pl.ds(k * CW, CW)

    def acts_cols(l_, hf):
        h = (1 - xh) if hf == 0 else xh
        return pl.ds(pl.multiple_of(l_ * D_BLK + h * HALF, 128), HALF)

    def out_cols(l_, t_):
        return pl.ds(pl.multiple_of(l_ * D_BLK + t_ * HALF, 128), HALF)

    load_g = [pltpu.make_async_copy(grads.at[:, cols(k)], G.at[k, l], lg_sem.at[k]) for k in range(NK)]
    load_w = pltpu.make_async_copy(wq, W, lw_sem.at[0])
    far_first = (4, 5, 3, 2, 6, 7, 1, 0)
    load_a = [
        [
            pltpu.make_async_copy(
                acts.at[:, acts_cols((l + o) % 8, hf)], AS.at[hf, (l + o) % 8], la_sem.at[hf, o]
            )
            for o in far_first
        ]
        for hf in range(2)
    ]

    load_g[0].start()
    for cp in load_a[0]:
        cp.start()
    for cp in load_g[1:]:
        cp.start()
    load_w.start()
    for cp in load_a[1]:
        cp.start()

    barrier = pltpu.get_barrier_semaphore()
    partners = [at_local((l + o) % 8) for o in range(1, 8)] + [dev_z[0], dev_z[1], dev_h, dev_x]
    for dev in partners:
        pl.semaphore_signal(barrier, inc=1, device_id=dev, device_id_type=MESH)
    pl.semaphore_wait(barrier, len(partners))

    def a_rows(first, size):
        return pl.ds(pl.multiple_of(first, 16), size)

    order = ((2, 0), (2, 1), (1, 0), (3, 0), (1, 1), (3, 1))

    def peer(off, flip, sign):
        yy = (y + off) % 4 if sign > 0 else (y + 4 - off) % 4
        return yy * 2 + (1 - c if flip else c)

    def send_acts(hf):
        for cp in load_a[hf]:
            cp.wait()
        for i, (off, flip) in enumerate(order):
            l_ = peer(off, flip, 1)
            r = a_rows(t * A_FAR, A_NEAR)
            send(AS.at[hf, l_, r], A.at[hf, l, r], a_ss.at[hf, i], a_rs.at[hf, i], at_local(l_))
        send(AS.at[hf, l_sib], A.at[hf, l], a_ss.at[hf, 6], a_rs.at[hf, 6], sib)

    def pass_acts(hf):
        for i, (off, flip) in enumerate(order):
            l_ = peer(off, flip, -1)
            arrived(A.at[hf, l_, a_rows(t * A_FAR, A_NEAR)], a_rs.at[hf, i])
            r = a_rows(t * A_NEAR, A_FAR)
            send(A.at[hf, l_, r], A.at[hf, l_, r], ax_ss.at[hf, i], ax_rs.at[hf, i], dev_x)

    def take_acts(hf):
        arrived(A.at[hf, l_sib], a_rs.at[hf, 6])
        for i, (off, flip) in enumerate(order):
            arrived(A.at[hf, peer(off, flip, -1), a_rows((1 - t) * A_NEAR, A_FAR)], ax_rs.at[hf, i])
        A[hf, l] = AS[hf, l]
        for i in range(8):
            AT[hf, :, i * TOK : (i + 1) * TOK] = A[hf, i].T

    def send_own(k):
        send(G.at[k, l], G.at[k, l], g_ss.at[k, 0], g_rs.at[k, 0], dev_yp)
        send(G.at[k, l], G.at[k, l], g_ss.at[k, 1], g_rs.at[k, 1], dev_ym)

    def relay(k):
        lm, lp = ym * 2 + c, yp * 2 + c
        low, high = pl.ds(0, TOK // 2), pl.ds(TOK // 2, TOK // 2)
        arrived(G.at[k, lm], g_rs.at[k, 0])
        send(G.at[k, lm, low], G.at[k, lm, low], g_ss.at[k, 2], g_rs.at[k, 2], dev_yp)
        arrived(G.at[k, lp], g_rs.at[k, 1])
        send(G.at[k, lp, high], G.at[k, lp, high], g_ss.at[k, 3], g_rs.at[k, 3], dev_ym)
        send(G.at[k, lm], G.at[k, lm], g_ss.at[k, 4], g_rs.at[k, 4], sib)
        send(G.at[k, lp], G.at[k, lp], g_ss.at[k, 5], g_rs.at[k, 5], sib)

    def near(k):
        arrived(G.at[k, ym * 2 + 1 - c], g_rs.at[k, 4])
        arrived(G.at[k, yp * 2 + 1 - c], g_rs.at[k, 5])

    def far(k):
        lf = y2 * 2 + c
        arrived(G.at[k, lf, pl.ds(0, TOK // 2)], g_rs.at[k, 2])
        arrived(G.at[k, lf, pl.ds(TOK // 2, TOK // 2)], g_rs.at[k, 3])
        send(G.at[k, lf], G.at[k, lf], g_ss.at[k, 6], g_rs.at[k, 6], sib)
        arrived(G.at[k, y2 * 2 + 1 - c], g_rs.at[k, 6])

    def unit_block(u):
        k, hf = divmod(u, 2)

        @pl.loop(0, CW // 256)
        def _(i):
            at = pl.ds(pl.multiple_of(i * 256, 128), 256)
            g = G[k, :, :, at].reshape(8 * TOK, 256)
            PZ[u, :, at] = jnp.dot(AT[hf], g, preferred_element_type=F32)

    def steps_of(u, d):
        return (1, 2, 3, 4) if u % 2 == d else (2, 3, 4)

    def z_step(u, s):
        if not 0 <= u < NU:
            return
        for d in range(2):
            if s not in steps_of(u, d):
                continue
            first = s == steps_of(u, d)[0]
            to = (z + 5 - s) % 8 if d == 0 else (z + 3 + s) % 8
            if not first:
                arrived(zr.at[u, d, s - 2], z_rs.at[u, d, s - 2])

            @pl.loop(0, ROWS // 16)
            def _(i):
                r = pl.ds(pl.multiple_of(i * 16, 16), 16)
                v = PZ[u, pl.ds(pl.multiple_of(to * ROWS + i * 16, 16), 16), :]
                if not first:
                    v = v + z_value(zr[u, d, s - 2, r, :])
                zs[u, d, s - 1, r, :] = z_code(v)

            send(zs.at[u, d, s - 1], zr.at[u, d, s - 1], z_ss.at[u, d, s - 1], z_rs.at[u, d, s - 1], dev_z[d])

    def z_final(u):
        if not 0 <= u < NU:
            return
        k, hf = divmod(u, 2)
        for d in range(2):
            arrived(zr.at[u, d, 3], z_rs.at[u, d, 3])
        if hf == 1:
            arrived(hr.at[k], h_rs.at[k])

        @pl.loop(0, ROWS // 16)
        def _(i):
            r = pl.ds(pl.multiple_of(i * 16, 16), 16)
            v = PZ[u, pl.ds(pl.multiple_of(z * ROWS + i * 16, 16), 16), :]
            v = v + z_value(zr[u, 0, 3, r, :]) + z_value(zr[u, 1, 3, r, :])
            if hf == 0:
                hs[k, r, :] = z_code(v)
            else:
                wo[k, r, :] = v + z_value(hr[k, r, :])

        if hf == 0:
            send(hs.at[k], hr.at[k], h_ss.at[k], h_rs.at[k], dev_h)
        else:
            store(wo.at[k], wg_out.at[0, :, cols(k)], lz_sem.at[k])

    def x_add(b, k):
        yb = chip[b]

        @pl.loop(0, 2)
        def _(i):
            p = lax.dot_general(
                G[k, yb * 2 + i], W[:, cols(k)], (((1,), (1,)), ((), ())), preferred_element_type=F32
            )
            r = pl.ds(pl.multiple_of(i * TOK, TOK), TOK)
            PX[b, r, :] = p if k == 0 else PX[b, r, :] + p

    NB = 2 * TOK

    def x_send(b):
        theirs = pl.ds(pl.multiple_of((1 - t) * HALF, 128), HALF)
        most = jnp.zeros((32, HALF), F32)
        for i in range(NB // 32):
            most = jnp.maximum(most, jnp.abs(PX[b, pl.ds(i * 32, 32), theirs]))
        most = jnp.maximum(jnp.max(most, axis=0, keepdims=True) * 1.01, 1e-30).astype(BF16)
        xs[b, pl.ds(NB, 16), :] = jnp.broadcast_to(most, (16, HALF))
        scale = X_TOP / most.astype(F32)

        @pl.loop(0, NB // 32)
        def _(i):
            r = pl.ds(pl.multiple_of(i * 32, 32), 32)
            xs[b, r, :] = power(PX[b, r, theirs] * scale, X_POWER).astype(BF16)

        send(xs.at[b], xr.at[b], x_ss.at[b], x_rs.at[b], dev_x)

    def x_final(b):
        arrived(xr.at[b], x_rs.at[b])
        mine = pl.ds(pl.multiple_of(t * HALF, 128), HALF)
        unscale = xr[b, pl.ds(NB, 16), :].astype(F32)[0:1] * (1.0 / X_TOP)

        @pl.loop(0, NB // 32)
        def _(i):
            r = pl.ds(pl.multiple_of(i * 32, 32), 32)
            v = PX[b, r, mine] + root(xr[b, r, :].astype(F32), X_POWER) * unscale
            fin[b, r, :] = v.astype(BF16)

        if b == 0:
            own = fin.at[0, pl.ds(pl.multiple_of(c * TOK, TOK), TOK)]
            other = fin.at[0, pl.ds(pl.multiple_of((1 - c) * TOK, TOK), TOK)]
            store(own, ag_out.at[:, out_cols(l, t)], lo_sem.at[0, 0])
            send(own, AO.at[t, l], ag_ss.at[0], ag_rs.at[0], dev_x)
            send(other, AO.at[t, l], o_ss.at[0], o_rs.at[1], sib)
        else:
            there = {1: 2, 2: 1, 3: 3}[b]
            for i in range(2):
                send(
                    fin.at[b, pl.ds(i * TOK, TOK)], AO.at[t, l],
                    o_ss.at[2 * b + i], o_rs.at[2 * there + c], at_local(chip[b] * 2 + i),
                )

    def x_share(b):
        for i in range(2):
            if b == 0 and i == 0:
                continue
            l_ = l_sib if b == 0 else chip[b] * 2 + i
            piece = AO.at[t, l_]
            arrived(piece, o_rs.at[2 * b + i])
            send(piece, piece, ag_ss.at[2 * b + i], ag_rs.at[2 * b + i], dev_x)
            store(piece, ag_out.at[:, out_cols(l_, t)], lo_sem.at[0, 2 * b + i])

    def x_take(b):
        for i in range(2):
            l_ = (l if i == 0 else l_sib) if b == 0 else chip[b] * 2 + i
            piece = AO.at[1 - t, l_]
            arrived(piece, ag_rs.at[2 * b + i])
            store(piece, ag_out.at[:, out_cols(l_, 1 - t)], lo_sem.at[1, 2 * b + i])

    load_g[0].wait()
    send_own(0)
    send_acts(0)
    for cp in load_g[1:]:
        cp.wait()
    send(G.at[:, l], G.at[:, l], sib_sem.at[0], sib_sem.at[1], sib)
    load_w.wait()
    arrived(G.at[:, l_sib], sib_sem.at[1])
    for k in range(NK):
        x_add(0, k)
    x_send(0)
    relay(0)
    send_own(1)
    pass_acts(0)
    send_acts(1)
    near(0)
    x_final(0)
    take_acts(0)
    far(0)
    for u in range(NU + 4):
        k, hf = divmod(u, 2)
        if hf == 0 and k + 2 < NK:
            send_own(k + 2)
        if u < NU:
            unit_block(u)
            z_step(u, 1)
        if u == 0:
            pass_acts(1)
        if hf == 0 and k + 1 < NK:
            relay(k + 1)
        if hf == 0 and k < NK - 1:
            for b in (1, 2, 3):
                x_add(b, k)
        if hf == 1 and k + 1 < NK:
            near(k + 1)
            if k + 1 == NK - 1:
                for b in (1, 2):
                    x_add(b, NK - 1)
                    x_send(b)
        z_step(u - 1, 2)
        if u == 0:
            take_acts(1)
        z_step(u - 2, 3)
        if hf == 1 and k + 1 < NK:
            far(k + 1)
            if k + 1 == NK - 1:
                x_add(3, NK - 1)
                x_send(3)
        z_step(u - 3, 4)
        z_final(u - 4)
        if u == 1:
            x_share(0)
        if u == NU - 2:
            x_final(1)
            x_final(2)
        if u == NU - 1:
            x_final(3)
            x_share(1)
            x_share(2)
        if u == NU:
            x_share(3)
            x_take(0)
    for b in (1, 2, 3):
        x_take(b)
    for cp in stores:
        cp.wait()
    for cp in started:
        cp.wait_send()


def on_device(acts, grad_q, weight_q):
    dma = pltpu.SemaphoreType.DMA
    return pl.pallas_call(
        kernel,
        out_shape=(
            jax.ShapeDtypeStruct((1, ROWS, QL), F32),
            jax.ShapeDtypeStruct((TOK, 8 * D_BLK), BF16),
        ),
        in_specs=[pl.BlockSpec(memory_space=pl.ANY)] * 3,
        out_specs=[pl.BlockSpec(memory_space=pl.ANY)] * 2,
        scratch_shapes=[
            pltpu.VMEM((D_BLK, QL), BF16),
            pltpu.VMEM((NK, 8, TOK, CW), BF16),
            pltpu.VMEM((2, 8, TOK, HALF), BF16),
            pltpu.VMEM((2, 8, TOK, HALF), BF16),
            pltpu.VMEM((2, HALF, 8 * TOK), BF16),
            pltpu.VMEM((NU, HALF, CW), F32),
            pltpu.VMEM((4, 2 * TOK, D_BLK), F32),
            pltpu.VMEM((NU, 2, 4, ROWS, CW), BF16),
            pltpu.VMEM((NU, 2, 4, ROWS, CW), BF16),
            pltpu.VMEM((4, 2 * TOK + 16, HALF), BF16),
            pltpu.VMEM((4, 2 * TOK + 16, HALF), BF16),
            pltpu.VMEM((NK, ROWS, CW), BF16),
            pltpu.VMEM((NK, ROWS, CW), BF16),
            pltpu.VMEM((NK, ROWS, CW), F32),
            pltpu.VMEM((4, 2 * TOK, HALF), BF16),
            pltpu.VMEM((2, 8, TOK, HALF), BF16),
            dma((NK,)),
            dma((1,)),
            dma((2, 8)),
            dma((2, 8)),
            dma((NK,)),
            dma((2,)),
            dma((2, 7)),
            dma((2, 7)),
            dma((2, 6)),
            dma((2, 6)),
            dma((NK, 7)),
            dma((NK, 7)),
            dma((NU, 2, 4)),
            dma((NU, 2, 4)),
            dma((4,)),
            dma((4,)),
            dma((NK,)),
            dma((NK,)),
            dma((8,)),
            dma((8,)),
            dma((8,)),
            dma((8,)),
        ],
        compiler_params=pltpu.CompilerParams(
            collective_id=0, has_side_effects=True, vmem_limit_bytes=58 * 2**20
        ),
        name="projection_backward",
    )(acts, grad_q, weight_q)


def solution(mesh):
    placed = (P(("node", "local"), None), P(("node", "local"), "tensor"), P("local", "tensor"))
    return jax.shard_map(
        on_device,
        mesh=mesh,
        in_specs=placed,
        out_specs=(P("local", "node", "tensor"), P(("node", "local"), None)),
        check_vma=False,
    )
```

time: 120 us -> 104 us (0.87)
  Pallas kernels: 114 us -> 98.7 us
    pallas_call x1, Pallas kernels: 114 us -> 98.7 us  [on_device(): pl.pallas_call(kernel, out_shape=(jax.ShapeDtypeStruct((1, ROWS, QL), F32...]
where the time goes in v2:
time: 104 us
  Pallas kernels  98.7 us (95%)
  local copies, waits for them, and re-layouts  4.61 us (4%)
    pallas_call x1, Pallas kernels, on_device(): pl.pallas_call(kernel, out_shape=(jax.ShapeDtypeStruct((1, ROWS, QL), F32...  98.7 us
    unnamed x2, local copies, waits for them, and re-layouts  4.61 us

profile of v2, /device:TPU:1, one launch (start us, length us, event | category | flops | bytes accessed | tf_op | source)
XLA Modules:
  0.0 104.0 jit_solution(455153090989291128)
XLA Ops:
  0.6 98.7 %projection_backward.1 = (f32[1,48,3072]{2,1,0:T(8,128)}, bf16[128,6144]{1,0:T(8,128)(2,1)}) custom-call(bf16[128,6144]{1,0:T(8,128)(2,1)} %acts.1, bf16[128,3072]{1,0:T(8,128)(2,1)} %grads.1, bf16[768,3072]{1,0:T(8,128)(2,1)} %wq.1), custom_call_target="tpu_custom_call" | custom-call | tf_op jit(solution)/shard_map/projection_backward/pallas_call | solution.py:395
  99.4 1.9 %copy.7 = f32[1,48,3072]{2,1,0:T(8,128)} copy(f32[1,48,3072]{2,1,0:T(8,128)} %get-tuple-element.4) | data formatting | bytes 1179648
  101.3 2.7 %copy.8 = bf16[128,6144]{1,0:T(8,128)(2,1)} copy(bf16[128,6144]{1,0:T(8,128)(2,1)} %get-tuple-element.5) | data formatting | bytes 3145728

commit v3 on v2

v3 whole, which is shorter than its diff:
```python
import jax
import jax.numpy as jnp
from jax import lax
from jax.experimental import pallas as pl
from jax.experimental.pallas import tpu as pltpu
from jax.sharding import PartitionSpec as P

MESH = pl.DeviceIdType.MESH
F32, BF16 = jnp.float32, jnp.bfloat16

TOK = 128
D_BLK = 768
HALF = 384
QL = 3072
WIDTHS = (384, 768, 768, 768, 384)
FIRST = tuple(sum(WIDTHS[:k]) for k in range(len(WIDTHS)))
NK = len(WIDTHS)
ROWS = 48
UNITS = ((0, 0), (1, 0), (0, 1), (1, 1), (2, 0), (2, 1), (3, 0), (4, 0), (3, 1), (4, 1))
NU = len(UNITS)

A_NEAR = 80
A_FAR = TOK - A_NEAR

Z_POWER, Z_SCALE = 5, 1024.0
X_POWER, X_TOP = 15, 300.0


def power(v, p):
    out, square = None, v
    while p:
        if p & 1:
            out = square if out is None else out * square
        p >>= 1
        if p:
            square = square * square
    return out


def root(code, p):
    a = jnp.abs(code)
    r = jnp.exp(jnp.log(jnp.maximum(a, 1e-38)) * (1.0 / p))
    r = jnp.where(a < 1e-37, 0.0, r)
    return jnp.where(code < 0, -r, r)


def z_code(v):
    return power(v * Z_SCALE, Z_POWER).astype(BF16)


def z_value(code):
    return root(code.astype(F32), Z_POWER) * (1.0 / Z_SCALE)


def kernel(
    acts, grads, wq, wg_out, ag_out,
    W, G, AS, A, AT, PZ, PX, zs, zr, xs, xr, hs, hr, wo, fin, AO,
    lg_sem, lw_sem, la_sem, lo_sem, lz_sem, sib_rs, a_ss, a_rs, ax_rs, g_ss, g_rs,
    z_ss, z_rs, x_ss, x_rs, h_ss, h_rs, o_ss, o_rs, ag_ss, ag_rs,
):
    t = lax.axis_index("tensor")
    n = lax.axis_index("node")
    l = lax.axis_index("local")
    xh, z = n // 8, n % 8
    y, c = l // 2, l % 2
    yp, ym, y2 = (y + 1) % 4, (y + 3) % 4, (y + 2) % 4
    chip = (y, yp, ym, y2)

    def at_local(l_):
        return (t, n, l_)

    l_sib = y * 2 + 1 - c
    sib = at_local(l_sib)
    dev_yp, dev_ym = at_local(yp * 2 + c), at_local(ym * 2 + c)
    dev_z = (
        (t, xh * 8 + (z + 1) % 8, l),
        (t, xh * 8 + (z + 7) % 8, l),
    )
    dev_h = (t, (1 - xh) * 8 + z, l)
    dev_x = (1 - t, n, l)


    def send(src, dst, ss, rs, dev):
        cp = pltpu.make_async_remote_copy(
            src_ref=src, dst_ref=dst, send_sem=ss, recv_sem=rs, device_id=dev, device_id_type=MESH
        )
        cp.start()

    def arrived(dst, rs):
        pltpu.make_async_remote_copy(
            src_ref=dst, dst_ref=dst, send_sem=rs, recv_sem=rs, device_id=sib, device_id_type=MESH
        ).wait_recv()

    def sent(total, ss):
        pltpu.make_async_remote_copy(
            src_ref=total, dst_ref=total, send_sem=ss, recv_sem=ss, device_id=sib, device_id_type=MESH
        ).wait_send()

    def store(src, dst, sem):
        pltpu.make_async_copy(src, dst, sem).start()

    def cols(k):
        return pl.ds(FIRST[k], WIDTHS[k])

    def acts_cols(l_, hf):
        h = (1 - xh) if hf == 0 else xh
        return pl.ds(pl.multiple_of(l_ * D_BLK + h * HALF, 128), HALF)

    def out_cols(l_, t_):
        return pl.ds(pl.multiple_of(l_ * D_BLK + t_ * HALF, 128), HALF)

    load_g = [pltpu.make_async_copy(grads.at[:, cols(k)], G[k].at[l], lg_sem.at[k]) for k in range(NK)]
    load_w = pltpu.make_async_copy(wq, W, lw_sem.at[0])
    far_first = (4, 5, 3, 2, 6, 7, 1, 0)
    load_a = [
        [
            pltpu.make_async_copy(
                acts.at[:, acts_cols((l + o) % 8, hf)], AS.at[hf, (l + o) % 8], la_sem.at[hf]
            )
            for o in far_first
        ]
        for hf in range(2)
    ]

    load_g[0].start()
    for cp in load_a[0]:
        cp.start()
    for cp in load_g[1:]:
        cp.start()
    load_w.start()
    for cp in load_a[1]:
        cp.start()

    barrier = pltpu.get_barrier_semaphore()
    partners = [at_local((l + o) % 8) for o in range(1, 8)] + [dev_z[0], dev_z[1], dev_h, dev_x]
    for dev in partners:
        pl.semaphore_signal(barrier, inc=1, device_id=dev, device_id_type=MESH)
    pl.semaphore_wait(barrier, len(partners))

    def a_rows(first, size):
        return pl.ds(pl.multiple_of(first, 16), size)

    order = ((2, 0), (2, 1), (1, 0), (3, 0), (1, 1), (3, 1))

    def peer(off, flip, sign):
        yy = (y + off) % 4 if sign > 0 else (y + 4 - off) % 4
        return yy * 2 + (1 - c if flip else c)

    def send_acts(hf, part):
        if part == 0:
            pltpu.make_async_copy(AS.at[hf], AS.at[hf], la_sem.at[hf]).wait()
        for i, (off, flip) in list(enumerate(order))[3 * part : 3 * part + 3]:
            l_ = peer(off, flip, 1)
            r = a_rows(t * A_FAR, A_NEAR)
            send(AS.at[hf, l_, r], A.at[hf, l, r], a_ss.at[hf], a_rs.at[hf, i], at_local(l_))
        if part == 0:
            send(AS.at[hf, l_sib], A.at[hf, l], a_ss.at[hf], a_rs.at[hf, 6], sib)

    def pass_acts(hf):
        for i, (off, flip) in enumerate(order):
            l_ = peer(off, flip, -1)
            arrived(A.at[hf, l_, a_rows(t * A_FAR, A_NEAR)], a_rs.at[hf, i])
            r = a_rows(t * A_NEAR, A_FAR)
            send(A.at[hf, l_, r], A.at[hf, l_, r], a_ss.at[hf], ax_rs.at[hf, i], dev_x)

    def turn(hf, l_, block):
        AT[hf, :, pl.ds(pl.multiple_of(l_ * TOK, TOK), TOK)] = block.T

    def take_acts(hf):
        turn(hf, l, AS[hf, l])
        arrived(A.at[hf, l_sib], a_rs.at[hf, 6])
        turn(hf, l_sib, A[hf, l_sib])
        for i, (off, flip) in enumerate(order):
            l_ = peer(off, flip, -1)
            arrived(A.at[hf, l_, a_rows((1 - t) * A_NEAR, A_FAR)], ax_rs.at[hf, i])
            turn(hf, l_, A[hf, l_])

    def send_own(k):
        own = G[k].at[l]
        send(own, own, g_ss.at[k], g_rs.at[k, 0], dev_yp)
        send(own, own, g_ss.at[k], g_rs.at[k, 1], dev_ym)

    def relay(k):
        lm, lp = ym * 2 + c, yp * 2 + c
        below, above = G[k].at[lm], G[k].at[lp]
        low, high = G[k].at[lm, pl.ds(0, TOK // 2)], G[k].at[lp, pl.ds(TOK // 2, TOK // 2)]
        arrived(below, g_rs.at[k, 0])
        send(low, low, g_ss.at[k], g_rs.at[k, 2], dev_yp)
        arrived(above, g_rs.at[k, 1])
        send(high, high, g_ss.at[k], g_rs.at[k, 3], dev_ym)
        send(below, below, g_ss.at[k], g_rs.at[k, 4], sib)
        send(above, above, g_ss.at[k], g_rs.at[k, 5], sib)

    def near(k):
        arrived(G[k].at[ym * 2 + 1 - c], g_rs.at[k, 4])
        arrived(G[k].at[yp * 2 + 1 - c], g_rs.at[k, 5])

    def far(k):
        lf = y2 * 2 + c
        arrived(G[k].at[lf, pl.ds(0, TOK // 2)], g_rs.at[k, 2])
        arrived(G[k].at[lf, pl.ds(TOK // 2, TOK // 2)], g_rs.at[k, 3])
        send(G[k].at[lf], G[k].at[lf], g_ss.at[k], g_rs.at[k, 6], sib)
        arrived(G[k].at[y2 * 2 + 1 - c], g_rs.at[k, 6])

    def send_shard():
        for k in range(NK):
            if k:
                load_g[k].wait()
            send(G[k].at[l], G[k].at[l], g_ss.at[k], sib_rs.at[k], sib)

    def take_shard():
        for k in range(NK):
            arrived(G[k].at[l_sib], sib_rs.at[k])

    def unit_block(u):
        k, hf = UNITS[u]

        tile = 384

        @pl.loop(0, WIDTHS[k] // tile)
        def _(i):
            at = pl.ds(pl.multiple_of(i * tile, 128), tile)
            g = G[k][:, :, at].reshape(8 * TOK, tile)
            PZ[u][:, at] = jnp.dot(AT[hf], g, preferred_element_type=F32)

    def steps_of(u, d):
        return (1, 2, 3, 4) if u % 2 == d else (2, 3, 4)

    def z_slot(u, d, s):
        return s - 1 if u % 2 == d else s + 2

    def z_step(u, s):
        if not 0 <= u < NU:
            return
        for d in range(2):
            if s not in steps_of(u, d):
                continue
            first = s == steps_of(u, d)[0]
            to = (z + 5 - s) % 8 if d == 0 else (z + 3 + s) % 8
            last, now = z_slot(u, d, s - 1), z_slot(u, d, s)
            if not first:
                arrived(zr[u].at[last], z_rs.at[u, last])

            @pl.loop(0, ROWS // 16)
            def _(i):
                r = pl.ds(pl.multiple_of(i * 16, 16), 16)
                v = PZ[u][pl.ds(pl.multiple_of(to * ROWS + i * 16, 16), 16), :]
                if not first:
                    v = v + z_value(zr[u][last, r, :])
                zs[u][now, r, :] = z_code(v)

            send(zs[u].at[now], zr[u].at[now], z_ss.at[u], z_rs.at[u, now], dev_z[d])

    def z_final(u):
        if not 0 <= u < NU:
            return
        k, hf = UNITS[u]
        low, high = z_slot(u, 0, 4), z_slot(u, 1, 4)
        arrived(zr[u].at[low], z_rs.at[u, low])
        arrived(zr[u].at[high], z_rs.at[u, high])
        if hf == 1:
            arrived(hr[k], h_rs.at[k])

        @pl.loop(0, ROWS // 16)
        def _(i):
            r = pl.ds(pl.multiple_of(i * 16, 16), 16)
            v = PZ[u][pl.ds(pl.multiple_of(z * ROWS + i * 16, 16), 16), :]
            v = v + z_value(zr[u][low, r, :]) + z_value(zr[u][high, r, :])
            if hf == 0:
                hs[k][r, :] = z_code(v)
            else:
                wo[k][r, :] = v + z_value(hr[k][r, :])

        if hf == 0:
            send(hs[k], hr[k], h_ss.at[k], h_rs.at[k], dev_h)
        else:
            store(wo[k], wg_out.at[0, :, cols(k)], lz_sem.at[k])

    def x_add(b, k):
        yb = chip[b]

        g = G[k][pl.ds(yb * 2, 2)].reshape(2 * TOK, WIDTHS[k])
        p = lax.dot_general(g, W[:, cols(k)], (((1,), (1,)), ((), ())), preferred_element_type=F32)
        PX[b] = p if k == 0 else PX[b] + p

    NB = 2 * TOK

    def x_send(b):
        theirs = pl.ds(pl.multiple_of((1 - t) * HALF, 128), HALF)
        most = jnp.zeros((32, HALF), F32)
        for i in range(NB // 32):
            most = jnp.maximum(most, jnp.abs(PX[b, pl.ds(i * 32, 32), theirs]))
        most = jnp.maximum(jnp.max(most, axis=0, keepdims=True) * 1.01, 1e-30).astype(BF16)
        xs[b, pl.ds(NB, 16), :] = jnp.broadcast_to(most, (16, HALF))
        scale = X_TOP / most.astype(F32)

        @pl.loop(0, NB // 32)
        def _(i):
            r = pl.ds(pl.multiple_of(i * 32, 32), 32)
            xs[b, r, :] = power(PX[b, r, theirs] * scale, X_POWER).astype(BF16)

        send(xs.at[b], xr.at[b], x_ss.at[0], x_rs.at[b], dev_x)

    def x_final(b):
        arrived(xr.at[b], x_rs.at[b])
        mine = pl.ds(pl.multiple_of(t * HALF, 128), HALF)
        unscale = xr[b, pl.ds(NB, 16), :].astype(F32)[0:1] * (1.0 / X_TOP)

        @pl.loop(0, NB // 32)
        def _(i):
            r = pl.ds(pl.multiple_of(i * 32, 32), 32)
            v = PX[b, r, mine] + root(xr[b, r, :].astype(F32), X_POWER) * unscale
            fin[b, r, :] = v.astype(BF16)

        if b == 0:
            own = fin.at[0, pl.ds(pl.multiple_of(c * TOK, TOK), TOK)]
            other = fin.at[0, pl.ds(pl.multiple_of((1 - c) * TOK, TOK), TOK)]
            store(own, ag_out.at[:, out_cols(l, t)], lo_sem.at[0])
            send(own, AO.at[t, l], ag_ss.at[0], ag_rs.at[0], dev_x)
            send(other, AO.at[t, l], o_ss.at[0], o_rs.at[1], sib)
        else:
            there = {1: 2, 2: 1, 3: 3}[b]
            for i in range(2):
                send(
                    fin.at[b, pl.ds(i * TOK, TOK)], AO.at[t, l],
                    o_ss.at[0], o_rs.at[2 * there + c], at_local(chip[b] * 2 + i),
                )

    def x_share(b):
        for i in range(2):
            if b == 0 and i == 0:
                continue
            l_ = l_sib if b == 0 else chip[b] * 2 + i
            piece = AO.at[t, l_]
            arrived(piece, o_rs.at[2 * b + i])
            send(piece, piece, ag_ss.at[0], ag_rs.at[2 * b + i], dev_x)
            store(piece, ag_out.at[:, out_cols(l_, t)], lo_sem.at[0])

    def x_take(b):
        for i in range(2):
            l_ = (l if i == 0 else l_sib) if b == 0 else chip[b] * 2 + i
            piece = AO.at[1 - t, l_]
            arrived(piece, ag_rs.at[2 * b + i])
            store(piece, ag_out.at[:, out_cols(l_, 1 - t)], lo_sem.at[0])

    load_g[0].wait()
    send_own(0)
    send_acts(0, 0)
    send_acts(0, 1)
    send_shard()
    relay(0)
    send_own(1)
    pass_acts(0)
    load_w.wait()
    take_shard()
    for i in range(NK):
        x_add(0, i)
    send_acts(1, 0)
    send_acts(1, 1)
    near(0)
    far(0)
    take_acts(0)
    unit_block(0)
    z_step(0, 1)
    relay(1)
    send_own(2)
    x_send(0)
    near(1)
    far(1)
    send_own(3)
    unit_block(1)
    z_step(1, 1)
    z_step(0, 2)
    pass_acts(1)
    x_final(0)
    relay(2)
    send_own(4)
    for b in (1, 2, 3):
        x_add(b, 0)
        x_add(b, 1)
    relay(3)
    take_acts(1)
    unit_block(2)
    z_step(2, 1)
    z_step(1, 2)
    z_step(0, 3)
    unit_block(3)
    z_step(3, 1)
    near(2)
    far(2)
    unit_block(4)
    z_step(4, 1)
    relay(4)
    z_step(2, 2)
    z_step(1, 3)
    unit_block(5)
    z_step(5, 1)
    z_step(0, 4)
    for b in (1, 2, 3):
        x_add(b, 2)
    z_step(3, 2)
    near(3)
    far(3)
    near(4)
    far(4)
    x_add(1, 3)
    x_add(1, 4)
    x_send(1)
    unit_block(6)
    z_step(6, 1)
    x_add(2, 3)
    x_add(2, 4)
    x_send(2)
    z_step(2, 3)
    z_step(1, 4)
    x_add(3, 3)
    x_add(3, 4)
    x_send(3)
    z_step(4, 2)
    z_step(3, 3)
    z_final(0)
    unit_block(7)
    z_step(7, 1)
    z_step(5, 2)
    z_step(2, 4)
    z_final(1)
    z_step(4, 3)
    z_step(3, 4)
    x_final(1)
    unit_block(8)
    z_step(8, 1)
    z_step(6, 2)
    z_step(5, 3)
    z_step(4, 4)
    x_share(0)
    x_final(2)
    unit_block(9)
    z_step(9, 1)
    z_step(7, 2)
    x_share(1)
    z_step(6, 3)
    z_step(5, 4)
    z_final(4)
    x_final(3)
    z_step(8, 2)
    z_step(9, 2)
    x_share(2)
    z_step(7, 3)
    z_step(6, 4)
    z_step(8, 3)
    z_step(9, 3)
    x_share(3)
    z_step(7, 4)
    z_final(2)
    z_final(3)
    z_step(8, 4)
    z_final(6)
    z_step(9, 4)
    z_final(7)
    z_final(5)
    x_take(0)
    x_take(1)
    x_take(2)
    x_take(3)
    z_final(8)
    z_final(9)
    for k in range(NK):
        pltpu.make_async_copy(wo[k], wg_out.at[0, :, cols(k)], lz_sem.at[k]).wait()
        sent(G[k].at[pl.ds(0, 7)], g_ss.at[k])
        sent(hs[k], h_ss.at[k])
    for hf in range(2):
        sent(A.at[hf, pl.ds(0, 7)], a_ss.at[hf])
    for u in range(NU):
        sent(zs[u], z_ss.at[u])
    sent(xs, x_ss.at[0])
    sent(AO.at[0, pl.ds(0, 7)], o_ss.at[0])
    sent(AO.at[0], ag_ss.at[0])
    pltpu.make_async_copy(AO, AO, lo_sem.at[0]).wait()


def move(a, b, out_a, out_b, va, vb, sems):
    steps = []
    for src, mid, dst, sem in (
        *((a.at[:, :, pl.ds(i * 1536, 1536)], va.at[:, :, pl.ds(i * 1536, 1536)], out_a.at[:, :, pl.ds(i * 1536, 1536)], i) for i in range(2)),
        *((b.at[pl.ds(i * 32, 32)], vb.at[pl.ds(i * 32, 32)], out_b.at[pl.ds(i * 32, 32)], 2 + i) for i in range(4)),
    ):
        steps.append((pltpu.make_async_copy(src, mid, sems.at[0, sem]), pltpu.make_async_copy(mid, dst, sems.at[1, sem])))
    for read, _ in steps:
        read.start()
    for read, write in steps:
        read.wait()
        write.start()
    for _, write in steps:
        write.wait()


def on_device(acts, grad_q, weight_q):
    dma = pltpu.SemaphoreType.DMA
    vmem = pltpu.VMEM
    units = [WIDTHS[k] for k, _ in UNITS]
    outs = (
        jax.ShapeDtypeStruct((1, ROWS, QL), F32),
        jax.ShapeDtypeStruct((TOK, 8 * D_BLK), BF16),
    )
    anywhere = pl.BlockSpec(memory_space=pl.ANY)
    results = pl.pallas_call(
        kernel,
        out_shape=outs,
        in_specs=[anywhere] * 3,
        out_specs=[anywhere] * 2,
        scratch_shapes=[
            vmem((D_BLK, QL), BF16),
            [vmem((8, TOK, w), BF16) for w in WIDTHS],
            vmem((2, 8, TOK, HALF), BF16),
            vmem((2, 8, TOK, HALF), BF16),
            vmem((2, HALF, 8 * TOK), BF16),
            [vmem((HALF, w), F32) for w in units],
            vmem((4, 2 * TOK, D_BLK), F32),
            [vmem((7, ROWS, w), BF16) for w in units],
            [vmem((7, ROWS, w), BF16) for w in units],
            vmem((4, 2 * TOK + 16, HALF), BF16),
            vmem((4, 2 * TOK + 16, HALF), BF16),
            [vmem((ROWS, w), BF16) for w in WIDTHS],
            [vmem((ROWS, w), BF16) for w in WIDTHS],
            [vmem((ROWS, w), F32) for w in WIDTHS],
            vmem((4, 2 * TOK, HALF), BF16),
            vmem((2, 8, TOK, HALF), BF16),
            dma((NK,)),
            dma((1,)),
            dma((2,)),
            dma((1,)),
            dma((NK,)),
            dma((NK,)),
            dma((2,)),
            dma((2, 7)),
            dma((2, 6)),
            dma((NK,)),
            dma((NK, 7)),
            dma((NU,)),
            dma((NU, 7)),
            dma((1,)),
            dma((4,)),
            dma((NK,)),
            dma((NK,)),
            dma((1,)),
            dma((8,)),
            dma((1,)),
            dma((8,)),
        ],
        compiler_params=pltpu.CompilerParams(
            collective_id=0, has_side_effects=True, vmem_limit_bytes=58 * 2**20
        ),
        name="projection_backward",
    )(acts, grad_q, weight_q)
    return pl.pallas_call(
        move,
        out_shape=outs,
        in_specs=[anywhere] * 2,
        out_specs=[anywhere] * 2,
        scratch_shapes=[vmem(outs[0].shape, F32), vmem(outs[1].shape, BF16), dma((2, 6))],
        name="results",
    )(*results)


def solution(mesh):
    placed = (P(("node", "local"), None), P(("node", "local"), "tensor"), P("local", "tensor"))
    return jax.shard_map(
        on_device,
        mesh=mesh,
        in_specs=placed,
        out_specs=(P("local", "node", "tensor"), P(("node", "local"), None)),
        check_vma=False,
    )
```

time: 104 us -> 99.3 us (0.955)
  local copies, waits for them, and re-layouts: 4.61 us -> 0 us
    unnamed x2 -> x0, local copies, waits for them, and re-layouts: 4.61 us -> none
    pallas_call x1 -> x2, Pallas kernels: 98.7 us -> 98.4 us  [the longest x1 96 us: on_device(): pl.pallas_call(kernel, out_shape=outs, in_specs=[anywhere] * 3, out_specs...]
where the time goes in v3:
time: 99.3 us; the launch traced here: 99.2 us
  Pallas kernels  98.4 us (99%)
    pallas_call x1, Pallas kernels, on_device(): pl.pallas_call(kernel, out_shape=outs, in_specs=[anywhere] * 3, out_specs...  96 us
    pallas_call x1, Pallas kernels, on_device(): pl.pallas_call(move, out_shape=outs, in_specs=[anywhere] * 2, out_specs=[...  2.41 us

profile of v3, /device:TPU:1, one launch (start us, length us, event | category | flops | bytes accessed | tf_op | source)
XLA Modules:
  0.0 99.2 jit_solution(1330750300559440425)
XLA Ops:
  0.6 96.0 %projection_backward.1 = (f32[1,48,3072]{2,1,0:T(8,128)}, bf16[128,6144]{1,0:T(8,128)(2,1)}) custom-call(bf16[128,6144]{1,0:T(8,128)(2,1)} %acts.1, bf16[128,3072]{1,0:T(8,128)(2,1)} %grads.1, bf16[768,3072]{1,0:T(8,128)(2,1)} %wq.1), custom_call_target="tpu_custom_call" | custom-call | tf_op jit(solution)/shard_map/projection_backward/pallas_call | solution.py:506
  96.7 2.4 %results.1 = (f32[1,48,3072]{2,1,0:T(8,128)}, bf16[128,6144]{1,0:T(8,128)(2,1)}) custom-call(f32[1,48,3072]{2,1,0:T(8,128)} %get-tuple-element.4.a, bf16[128,6144]{1,0:T(8,128)(2,1)} %get-tuple-element.5.b), custom_call_target="tpu_custom_call" | custom-call | tf_op jit(solution)/shard_map/results/pallas_call | solution.py:555

commit v4 on v3

--- a/solution.py
+++ b/solution.py
@@ -19,7 +19,7 @@
 UNITS = ((0, 0), (1, 0), (0, 1), (1, 1), (2, 0), (2, 1), (3, 0), (4, 0), (3, 1), (4, 1))
 NU = len(UNITS)
 
-A_NEAR = 80
+A_NEAR = 64
 A_FAR = TOK - A_NEAR
 
 Z_POWER, Z_SCALE = 5, 1024.0
@@ -386,11 +386,11 @@
     z_step(0, 3)
     unit_block(3)
     z_step(3, 1)
+    relay(4)
     near(2)
     far(2)
     unit_block(4)
     z_step(4, 1)
-    relay(4)
     z_step(2, 2)
     z_step(1, 3)
     unit_block(5)

time: 99.3 us -> 99 us (level)
  no operation moved by 1% of the time
where the time goes in v4:
time: 99 us; the launch traced here: 98.9 us
  Pallas kernels  98.1 us (99%)
    pallas_call x1, Pallas kernels, on_device(): pl.pallas_call(kernel, out_shape=outs, in_specs=[anywhere] * 3, out_specs...  95.7 us
    pallas_call x1, Pallas kernels, on_device(): pl.pallas_call(move, out_shape=outs, in_specs=[anywhere] * 2, out_specs=[...  2.41 us

profile of v4, /device:TPU:1, one launch (start us, length us, event | category | flops | bytes accessed | tf_op | source)
XLA Modules:
  0.0 98.9 jit_solution(13379030868599591012)
XLA Ops:
  0.6 95.7 %projection_backward.1 = (f32[1,48,3072]{2,1,0:T(8,128)}, bf16[128,6144]{1,0:T(8,128)(2,1)}) custom-call(bf16[128,6144]{1,0:T(8,128)(2,1)} %acts.1, bf16[128,3072]{1,0:T(8,128)(2,1)} %grads.1, bf16[768,3072]{1,0:T(8,128)(2,1)} %wq.1), custom_call_target="tpu_custom_call" | custom-call | tf_op jit(solution)/shard_map/projection_backward/pallas_call | solution.py:506
  96.3 2.4 %results.1 = (f32[1,48,3072]{2,1,0:T(8,128)}, bf16[128,6144]{1,0:T(8,128)(2,1)}) custom-call(f32[1,48,3072]{2,1,0:T(8,128)} %get-tuple-element.4.a, bf16[128,6144]{1,0:T(8,128)(2,1)} %get-tuple-element.5.b), custom_call_target="tpu_custom_call" | custom-call | tf_op jit(solution)/shard_map/results/pallas_call | solution.py:555
